TPU v7x, 32 devices: a whole 2x2x4 slice. The times are simulated.
32 devices in a mesh: inner: 8 (over y, x, core), outer: 4 (over z).
Axes of the slice: x: 2, y: 2, z: 4, core: 2. Of those that a mesh axis runs over, the one named last changes fastest.
Arguments:
- grad_first: bfloat16 [4, 8, 8, 4, 6, 128], P('outer', 'inner'), may hold values from -1 to 1
- grad_second: bfloat16 [4, 8, 8, 4, 6, 128], P('outer', 'inner'), may hold values from -1 to 1
- master: float32 [2, 8, 4, 6, 128], P(None, 'inner', 'outer'), may hold values from -0.12 to 0.12
- first_moment: float32 [2, 8, 4, 6, 128], P(None, 'inner', 'outer'), may hold values from -1.2 to 1.2
- second_moment: float32 [2, 8, 4, 6, 128], P(None, 'inner', 'outer'), may hold values from 0.01 to 1
Outputs:
- new_master: float32 [2, 8, 4, 6, 128], P(None, 'inner', 'outer')
- new_first: float32 [2, 8, 4, 6, 128], P(None, 'inner', 'outer')
- new_second: float32 [2, 8, 4, 6, 128], P(None, 'inner', 'outer')
- weight_codes: bfloat16 [2, 8, 4, 6, 128], P(None, None, 'outer')
- weight_scales: bfloat16 [2, 8, 4, 6], P(None, None, 'outer')
All inputs are finite; a program needn't handle non-finite values.
Results may differ from a plain program's by a relative error of at most 0.012.
Values may be sent and summed in bfloat16 or wider, within the bound.
A program may use at most 64 MiB of HBM per device.

v0:
```python
import jax
import jax.numpy as jnp
from jax import lax
from jax.sharding import PartitionSpec as P

EPSILON = 1e-06
CODE_RANGE = 448.0
BETA_ONE = 0.9
BETA_TWO = 0.95
LEARN_RATE = 0.01
WEIGHT_DECAY = 0.1
ADAM_EPSILON = 1e-08
steps_done = 10.0


def quantize(values):
    widened = values.astype(jnp.float32)
    block_scale = ((jnp.max(jnp.abs(widened), axis=-1) + EPSILON) / CODE_RANGE).astype(jnp.bfloat16)
    quant_codes = (widened / block_scale.astype(jnp.float32)[..., None]).astype(jnp.bfloat16)
    return (quant_codes, block_scale)


def restore(quant_codes, block_scale):
    return quant_codes.astype(jnp.float32) * block_scale.astype(jnp.float32)[..., None]


def adamw(reduced, params, first, second):
    first_next = BETA_ONE * first + (1.0 - BETA_ONE) * reduced
    second_next = BETA_TWO * second + (1.0 - BETA_TWO) * reduced * reduced
    first_hat = first_next / (1.0 - BETA_ONE**steps_done)
    second_hat = second_next / (1.0 - BETA_TWO**steps_done)
    params_next = params - LEARN_RATE * (
        first_hat / (jnp.sqrt(second_hat) + ADAM_EPSILON) + WEIGHT_DECAY * params
    )
    return (params_next, first_next, second_next)


def local(grad_first, grad_second, master, first_moment, second_moment):
    masters, firsts, seconds, all_codes, all_scales = ([], [], [], [], [])
    for bucket, gradient in enumerate((grad_first, grad_second)):
        codes_one, scale_one = quantize(gradient[0, 0])
        summed = lax.psum_scatter(
            restore(codes_one, scale_one), "inner", scatter_dimension=0, tiled=True
        )[0]
        codes_two, scale_two = quantize(summed)
        reduced = lax.psum_scatter(
            restore(codes_two, scale_two), "outer", scatter_dimension=0, tiled=True
        )[0]
        params_next, first_next, second_next = adamw(
            reduced, master[bucket, 0, 0], first_moment[bucket, 0, 0], second_moment[bucket, 0, 0]
        )
        weight_code, weight_scale = quantize(params_next)
        group_codes, group_scales = (
            lax.all_gather(weight_code[None], "inner", axis=0, tiled=True),
            lax.all_gather(weight_scale[None], "inner", axis=0, tiled=True),
        )
        masters.append(params_next)
        firsts.append(first_next)
        seconds.append(second_next)
        all_codes.append(group_codes)
        all_scales.append(group_scales)
    return (
        jnp.stack(masters)[:, None, None],
        jnp.stack(firsts)[:, None, None],
        jnp.stack(seconds)[:, None, None],
        jnp.stack(all_codes)[:, :, None],
        jnp.stack(all_scales)[:, :, None],
    )


def solution(mesh):
    return jax.shard_map(
        local,
        mesh=mesh,
        in_specs=(
            P("outer", "inner", None, None, None, None),
            P("outer", "inner", None, None, None, None),
            P(None, "inner", "outer", None, None),
            P(None, "inner", "outer", None, None),
            P(None, "inner", "outer", None, None),
        ),
        out_specs=(
            P(None, "inner", "outer", None, None),
            P(None, "inner", "outer", None, None),
            P(None, "inner", "outer", None, None),
            P(None, None, "outer", None, None),
            P(None, None, "outer", None),
        ),
        check_vma=False,
    )
```

profile of v0, /device:TPU:0, one launch (start us, length us, event | category | flops | bytes accessed | tf_op | source)
XLA Modules:
  0.0 146.6 jit_solution(9461905877052382310)
XLA Ops:
  7.2 0.0 copy-start
  7.2 0.0 reduce-scatter.3.cloned.1.call-start
  7.2 0.9 fusion
  8.2 0.0 copy-done
  8.2 0.7 convert_multiply_fusion.1
  8.9 0.0 copy-start.1
  8.9 0.0 reduce-scatter.3.cloned.1.call-update
  9.0 0.0 reduce-scatter.5.cloned.1.call-start
  9.0 0.7 copy-done.1
  9.7 0.1 fusion.2
  9.9 0.8 convert_multiply_fusion
  10.6 0.0 reduce-scatter.5.cloned.1.call-update
  10.7 0.0 copy-start.4
  10.7 0.7 copy-done.4
  11.4 0.0 copy-start.5
  11.4 0.0 copy-start.6
  11.4 0.7 copy-done.5
  12.0 0.0 copy-done.6
  12.1 0.0 copy-start.8
  12.1 0.7 copy-done.8
  12.7 0.6 dynamic-slice.2
  13.3 0.0 copy-start.7
  13.3 0.7 copy-done.7
  14.0 0.6 dynamic-slice
  15.2 31.9 %reduce-scatter.3.cloned.1.call-done = f32[1,4,6,128]{3,2,1,0:T(8,128)} async-done(((f32[8,4,6,128]{3,2,1,0:T(8,128)}), f32[1,4,6,128]{3,2,1,0:T(8,128)}) %reduce-scatter.3.cloned.1.call-update) | async-done | bytes 12304 | tf_op jit(solution)/shard_map/reduce_scatter | solution.py:42
  47.1 0.8 fusion.6
  47.9 0.0 copy-start.2
  47.9 35.9 %reduce-scatter.5.cloned.1.call-done = f32[1,4,6,128]{3,2,1,0:T(8,128)} async-done(((f32[8,4,6,128]{3,2,1,0:T(8,128)}), f32[1,4,6,128]{3,2,1,0:T(8,128)}) %reduce-scatter.5.cloned.1.call-update) | async-done | bytes 12304 | tf_op jit(solution)/shard_map/reduce_scatter | solution.py:42
  83.8 0.8 fusion.4
  84.6 0.0 copy-done.2
  84.6 0.0 copy-start.3
  84.6 0.1 convert_multiply_fusion.3
  84.7 0.6 copy-done.3
  85.3 0.1 convert_multiply_fusion.2
  85.4 19.0 %all-reduce.4 = (f32[4,6,128]{2,1,0:T(8,128)S(1)}, f32[4,6,128]{2,1,0:T(8,128)S(1)}) all-reduce(f32[4,6,128]{2,1,0:T(8,128)S(1)} %convert_multiply_fusion.2, f32[4,6,128]{2,1,0:T(8,128)S(1)} %convert_multiply_fusion.3), channel_id=7, replica_groups=mesh['inner'=8,'outer'=4] {'outer'}, use_global_device_ids=true, to_apply=%region_7.0.clone | all-reduce | flops 6144 | bytes 49152
  104.4 0.8 fusion.21
  105.2 0.8 fusion.27
  106.0 0.2 dynamic-update-slice
  106.2 0.2 dynamic-update-slice.1
  106.5 11.8 %all-reduce.5 = (bf16[48]{0:T(256)(128)(2,1)S(1)}, bf16[48]{0:T(256)(128)(2,1)S(1)}) all-reduce(bf16[48]{0:T(256)(128)(2,1)S(1)} %dynamic-update-slice.1, bf16[48]{0:T(256)(128)(2,1)S(1)} %dynamic-update-slice), channel_id=3, replica_groups=mesh['inner'=8,'outer'=4] {'inner'}, use_global_device_ids=true, to_apply=%add.1 | all-reduce | flops 96 | bytes 384
  118.2 0.1 stack.39
  118.3 0.1 stack.40
  118.4 0.7 copy.67
  119.1 0.7 divide_convert_fusion.1
  119.8 8.9 %all_gather.12 = bf16[8,6,128]{2,1,0:T(8,128)(2,1)S(1)} all-gather(bf16[1,6,128]{2,1,0:T(8,128)(2,1)S(1)} %get-tuple-element.19), channel_id=1, replica_groups=mesh['inner'=8,'outer'=4] {'inner'}, dimensions={0}, use_global_device_ids=true | all-gather | bytes 13824 | tf_op jit(solution)/shard_map/all_gather | solution.py:54
  128.7 0.7 divide_convert_fusion
  129.4 7.9 %all_gather.13 = bf16[8,6,128]{2,1,0:T(8,128)(2,1)S(1)} all-gather(bf16[1,6,128]{2,1,0:T(8,128)(2,1)S(1)} %get-tuple-element.23), channel_id=1, replica_groups=mesh['inner'=8,'outer'=4] {'inner'}, dimensions={0}, use_global_device_ids=true | all-gather | bytes 13824 | tf_op jit(solution)/shard_map/all_gather | solution.py:54
  137.3 0.6 copy.71
  138.0 0.6 copy.70
  138.6 0.6 copy.69
  139.2 0.6 copy.68
  (15 shorter events, 0.1 us)
Async XLA Ops:
  7.2 1.0 copy-start
  7.2 39.9 %reduce-scatter.3.cloned.1.call-start = ((), (), s32[]{:S(2)}) async-start(), calls=%async_computation.2 | async-start | bytes 147456 | tf_op jit(solution)/shard_map/reduce_scatter | solution.py:42
  8.9 0.8 copy-start.1
  9.0 74.8 %reduce-scatter.5.cloned.1.call-start = ((), (), s32[]{:S(2)}) async-start(), calls=%async_computation.3 | async-start | bytes 147456 | tf_op jit(solution)/shard_map/reduce_scatter | solution.py:42
  10.7 0.7 copy-start.4
  11.4 0.7 copy-start.5
  11.4 0.7 copy-start.6
  12.1 0.7 copy-start.8
  13.3 0.7 copy-start.7
  47.9 36.7 %copy-start.2 = (f32[1,4,6,128]{3,2,1,0:T(8,128)S(1)}, f32[1,4,6,128]{3,2,1,0:T(8,128)}, u32[]{:S(2)}) copy-start(f32[1,4,6,128]{3,2,1,0:T(8,128)} %reduce-scatter.3.cloned.1.call-done) | copy-start | bytes 36868
  84.6 0.7 copy-start.3
Sparse Core Ops, SparseCore 0:
  11.0 36.0 reduce-scatter.2
  50.4 33.3 reduce-scatter.4
where the time goes:
time: 147 us
  waiting for transfers between devices  67.8 us (46%)
  blocking collectives  47.6 us (32%)
  between operations  14.8 us (10%)
  local copies, waits for them, and re-layouts  8.97 us (6%)
  other arithmetic  7.37 us (5%)
    reduce_scatter x2, waiting for transfers between devices, local(): lax.psum_scatter(restore(codes_one, scale_one), 'inner', scatter_dimensio...  67.8 us
    unnamed x2, blocking collectives  30.8 us
    all_gather x2, blocking collectives, local(): lax.all_gather(weight_code[None], 'inner', axis=0, tiled=True)  16.8 us
    unnamed x28, local copies, waits for them, and re-layouts  8.11 us
    reduce_max x6, other arithmetic, quantize(): jnp.max(jnp.abs(widened), axis=-1) + EPSILON  4.21 us
  transfers between devices with their start and end apart: 2, of which 2 were waited for; matrix products, arithmetic and copies ran while one was open for 2% of the time, Pallas kernels for 0%

commit v1 on v0

v1 whole, which is shorter than its diff:
```python
import functools

import jax
import jax.numpy as jnp
from jax import lax
from jax.experimental import pallas as pl
from jax.experimental.pallas import tpu as pltpu
from jax.sharding import PartitionSpec as P

EPSILON = 1e-06
CODE_RANGE = 448.0
BETA_ONE = 0.9
BETA_TWO = 0.95
LEARN_RATE = 0.01
WEIGHT_DECAY = 0.1
ADAM_EPSILON = 1e-08
steps_done = 10.0
MESH = pl.DeviceIdType.MESH


def quantize(widened):
    most = jnp.max(jnp.abs(widened), axis=-1, keepdims=True)
    scale = ((most + EPSILON) / CODE_RANGE).astype(jnp.bfloat16).astype(jnp.float32)
    codes = (widened / scale).astype(jnp.bfloat16).astype(jnp.float32)
    return codes, scale


def requantized(widened):
    codes, scale = quantize(widened)
    return codes * scale


def adamw(reduced, params, first, second):
    first_next = BETA_ONE * first + (1.0 - BETA_ONE) * reduced
    second_next = BETA_TWO * second + (1.0 - BETA_TWO) * reduced * reduced
    first_hat = first_next / (1.0 - BETA_ONE**steps_done)
    second_hat = second_next / (1.0 - BETA_TWO**steps_done)
    params_next = params - LEARN_RATE * (
        first_hat / (jnp.sqrt(second_hat) + ADAM_EPSILON) + WEIGHT_DECAY * params
    )
    return (params_next, first_next, second_next)


def loop(count, body, carry):
    if count <= 8:
        for step in range(1, count):
            carry = body(step, carry)
        return carry
    return lax.fori_loop(1, count, body, carry)


def kernel(
    n_inner, n_outer, rows, padded,
    grad_first, grad_second, master, first_moment, second_moment,
    new_master, new_first, new_second, weight_codes, weight_scales,
    stage, terms, partial, sums, packed, state,
    load_sem, send_one, recv_one, send_two, recv_two, send_three, recv_three,
):
    inner = lax.axis_index("inner")
    outer = lax.axis_index("outer")
    both = 2 * rows
    width = stage.shape[-1]

    def inner_peer(step):
        return lax.rem(inner + step, n_inner)

    def outer_peer(step):
        return lax.rem(outer + step, n_outer)

    barrier = pltpu.get_barrier_semaphore()

    def greet_inner(step, carry):
        pl.semaphore_signal(barrier, inc=1, device_id={"inner": inner_peer(step)}, device_id_type=MESH)
        return carry

    def greet_outer(step, carry):
        pl.semaphore_signal(barrier, inc=1, device_id={"outer": outer_peer(step)}, device_id_type=MESH)
        return carry

    loop(n_inner, greet_inner, 0)
    loop(n_outer, greet_outer, 0)
    grads = [
        pltpu.make_async_copy(ref, stage.at[:, bucket], load_sem.at[bucket])
        for bucket, ref in enumerate((grad_first, grad_second))
    ]
    states = [
        pltpu.make_async_copy(ref, state.at[place], load_sem.at[2 + place])
        for place, ref in enumerate((master, first_moment, second_moment))
    ]
    for copy in grads + states:
        copy.start()
    for copy in grads:
        copy.wait()
    pl.semaphore_wait(barrier, n_inner - 1 + n_outer - 1)

    def term_copy(step):
        return pltpu.make_async_remote_copy(
            src_ref=stage.at[inner_peer(step)],
            dst_ref=terms.at[step],
            send_sem=send_one.at[step],
            recv_sem=recv_one.at[step],
            device_id={"inner": inner_peer(step)},
            device_id_type=MESH,
        )

    def send_term(step, carry):
        term_copy(step).start()
        return carry

    loop(n_inner, send_term, 0)
    total = requantized(stage[inner].astype(jnp.float32))

    def add_term(step, total):
        term_copy(step).wait_recv()
        return total + requantized(terms[step].astype(jnp.float32))

    total = loop(n_inner, add_term, total).reshape(both, n_outer, width)
    for group in range(n_outer):
        partial[group] = total[:, group]

    def sum_copy(step):
        return pltpu.make_async_remote_copy(
            src_ref=partial.at[outer_peer(step)],
            dst_ref=sums.at[step],
            send_sem=send_two.at[step],
            recv_sem=recv_two.at[step],
            device_id={"outer": outer_peer(step)},
            device_id_type=MESH,
        )

    def send_sum(step, carry):
        sum_copy(step).start()
        return carry

    loop(n_outer, send_sum, 0)
    reduced = requantized(partial[outer])
    for copy in states:
        copy.wait()
    params, first, second = (state[place, :, 0] for place in range(3))

    def add_sum(step, reduced):
        sum_copy(step).wait_recv()
        return reduced + requantized(sums[step])

    reduced = loop(n_outer, add_sum, reduced)

    params_next, first_next, second_next = adamw(reduced, params, first, second)
    codes, scale = quantize(params_next)
    lane = lax.broadcasted_iota(jnp.int32, (both, width), 1)
    row = lax.broadcasted_iota(jnp.int32, (both, width), 0)
    across = [
        jnp.sum(jnp.where(lane + bucket * rows == row, jnp.where(lane < rows, scale, 0.0), 0.0), axis=0, keepdims=True)
        for bucket in range(2)
    ]
    fill = jnp.zeros((padded - both - 2, width), jnp.float32)
    packed[inner] = jnp.concatenate([codes] + across + [fill], axis=0).astype(jnp.bfloat16)

    def weight_copy(step):
        return pltpu.make_async_remote_copy(
            src_ref=packed.at[inner],
            dst_ref=packed.at[inner],
            send_sem=send_three.at[step],
            recv_sem=recv_three.at[step],
            device_id={"inner": inner_peer(step)},
            device_id_type=MESH,
        )

    def send_weight(step, carry):
        weight_copy(step).start()
        return carry

    loop(n_inner, send_weight, 0)
    new_master[:, 0] = params_next
    new_first[:, 0] = first_next
    new_second[:, 0] = second_next

    def finish_terms(step, carry):
        term_copy(step).wait_send()
        return carry

    def finish_sums(step, carry):
        sum_copy(step).wait_send()
        return carry

    def finish_weights(step, carry):
        weight_copy(step).wait()
        return carry

    loop(n_inner, finish_terms, 0)
    loop(n_outer, finish_sums, 0)
    loop(n_inner, finish_weights, 0)
    gathered = packed[...].astype(jnp.float32)
    for place in range(both):
        weight_codes[place] = gathered[:, place].astype(jnp.bfloat16)
    for bucket in range(2):
        turned = jnp.transpose(gathered[:, both + bucket])
        weight_scales[:, bucket] = turned[:rows].astype(jnp.bfloat16)


def place_kernel(*refs):
    sources, results, sem = refs[:5], refs[5:10], refs[10]
    copies = [
        pltpu.make_async_copy(source, result, sem.at[place])
        for place, (source, result) in enumerate(zip(sources, results))
    ]
    for copy in copies:
        copy.start()
    for copy in copies:
        copy.wait()


def local(n_inner, n_outer, grad_first, grad_second, master, first_moment, second_moment):
    rows, width = grad_first.shape[-2:]
    both = 2 * rows
    padded = 16 * ((both + 2 + 15) // 16)
    owned = jax.ShapeDtypeStruct((both, 1, width), jnp.float32)
    shapes = (
        owned,
        owned,
        owned,
        jax.ShapeDtypeStruct((both, n_inner, width), jnp.bfloat16),
        jax.ShapeDtypeStruct((rows, 2, n_inner), jnp.bfloat16),
    )
    hbm = pl.BlockSpec(memory_space=pl.ANY)
    vmem = pl.BlockSpec(memory_space=pltpu.VMEM)
    dma = pltpu.SemaphoreType.DMA
    results = pl.pallas_call(
        functools.partial(kernel, n_inner, n_outer, rows, padded),
        out_shape=shapes,
        in_specs=[pl.BlockSpec(memory_space=pltpu.HBM)] * 5,
        out_specs=(vmem,) * 5,
        scratch_shapes=[
            pltpu.VMEM((n_inner, 2, rows, n_outer, width), jnp.bfloat16),
            pltpu.VMEM((n_inner, 2, rows, n_outer, width), jnp.bfloat16),
            pltpu.VMEM((n_outer, both, width), jnp.float32),
            pltpu.VMEM((n_outer, both, width), jnp.float32),
            pltpu.VMEM((n_inner, padded, width), jnp.bfloat16),
            pltpu.VMEM((3, both, 1, width), jnp.float32),
            dma((5,)),
            dma((n_inner,)),
            dma((n_inner,)),
            dma((n_outer,)),
            dma((n_outer,)),
            dma((n_inner,)),
            dma((n_inner,)),
        ],
        compiler_params=pltpu.CompilerParams(
            collective_id=0, has_side_effects=True
        ),
        name="reduce_update_gather",
    )(
        jnp.swapaxes(grad_first[0, 0], 1, 2),
        jnp.swapaxes(grad_second[0, 0], 1, 2),
        master.reshape(both, 1, width),
        first_moment.reshape(both, 1, width),
        second_moment.reshape(both, 1, width),
    )
    results = pl.pallas_call(
        place_kernel,
        out_shape=shapes,
        in_specs=[vmem] * 5,
        out_specs=(hbm,) * 5,
        scratch_shapes=[dma((5,))],
        name="place_results",
    )(*results)
    new_master, new_first, new_second, weight_codes, weight_scales = results
    state_shape = (2, 1, 1, rows, width)
    return (
        new_master.reshape(state_shape),
        new_first.reshape(state_shape),
        new_second.reshape(state_shape),
        jnp.swapaxes(weight_codes.reshape(2, rows, n_inner, width), 1, 2)[:, :, None],
        jnp.transpose(weight_scales, (1, 2, 0))[:, :, None],
    )


def solution(mesh):
    return jax.shard_map(
        functools.partial(local, mesh.shape["inner"], mesh.shape["outer"]),
        mesh=mesh,
        in_specs=(
            P("outer", "inner", None, None, None, None),
            P("outer", "inner", None, None, None, None),
            P(None, "inner", "outer", None, None),
            P(None, "inner", "outer", None, None),
            P(None, "inner", "outer", None, None),
        ),
        out_specs=(
            P(None, "inner", "outer", None, None),
            P(None, "inner", "outer", None, None),
            P(None, "inner", "outer", None, None),
            P(None, None, "outer", None, None),
            P(None, None, "outer", None),
        ),
        check_vma=False,
    )
```

time: 147 us -> 19.6 us (0.13)
  waiting for transfers between devices: 67.8 us -> 0 us
  blocking collectives: 47.6 us -> 0 us
  Pallas kernels: 0 us -> 18.7 us
  between operations: 14.8 us -> 0.64 us
  local copies, waits for them, and re-layouts: 8.97 us -> 0 us
  other arithmetic: 7.37 us -> 0 us
    reduce_scatter x2 -> x0, waiting for transfers between devices: 67.8 us -> none  [local(): lax.psum_scatter(restore(codes_one, scale_one), 'inner', scatter_dimensio...]
    unnamed x2 -> x0, blocking collectives: 30.8 us -> none
    pallas_call x0 -> x2, Pallas kernels: none -> 18.7 us  [the longest x1 17.3 us: local(): pl.pallas_call(functools.partial(kernel, n_inner, n_outer, rows, padded),...]
    all_gather x2 -> x0, blocking collectives: 16.8 us -> none  [local(): lax.all_gather(weight_code[None], 'inner', axis=0, tiled=True)]
    unnamed x28 -> x0, local copies, waits for them, and re-layouts: 8.11 us -> none
    reduce_max x6 -> x0, other arithmetic: 4.21 us -> none  [quantize(): jnp.max(jnp.abs(widened), axis=-1) + EPSILON]
    mul x4 -> x0, other arithmetic: 1.66 us -> none  [restore(): quant_codes.astype(jnp.float32) * block_scale.astype(jnp.float32)[..., None]]
  transfers between devices with their start and end apart: 2 -> 0, of which waited for: 2 -> 0; matrix products, arithmetic and copies ran while one was open for 2% -> 0% of each run, Pallas kernels for 0% -> 0%
where the time goes in v1:
time: 19.6 us; the launch traced here: 19.4 us
  Pallas kernels  18.7 us (95%)
  between operations  0.64 us (3%)
    pallas_call x1, Pallas kernels, local(): pl.pallas_call(functools.partial(kernel, n_inner, n_outer, rows, padded),...  17.3 us
    pallas_call x1, Pallas kernels, local(): pl.pallas_call(place_kernel, out_shape=shapes, in_specs=[vmem] * 5, out_s...  1.42 us

profile of v1, /device:TPU:0, one launch (start us, length us, event | category | flops | bytes accessed | tf_op | source)
XLA Modules:
  0.0 19.4 jit_solution(13402100779370723458)
XLA Ops:
  0.6 17.3 %reduce_update_gather.1 = (f32[12,1,128]{2,1,0:T(1,128)}, f32[12,1,128]{2,1,0:T(1,128)}, f32[12,1,128]{2,1,0:T(1,128)}, bf16[12,8,128]{2,1,0:T(8,128)(2,1)}, bf16[6,2,8]{2,1,0:T(2,128)(2,1)}) custom-call(bf16[8,6,4,128]{3,2,1,0:T(4,128)(2,1)} %bitcast.26, bf16[8,6,4,128]{3,2,1,0:T(4,128)(2,1)} %bitcast.27, f32[12,1,128]{2,1,0:T(1,128)} %bitcast.28, ...), custom_call_target="tpu_custom_call" | custom-call | tf_op jit(solution)/shard_map/reduce_update_gather/pallas_call | solution.py:227
  17.9 1.4 %place_results.1 = (f32[12,1,128]{2,1,0:T(1,128)}, f32[12,1,128]{2,1,0:T(1,128)}, f32[12,1,128]{2,1,0:T(1,128)}, bf16[12,8,128]{2,1,0:T(8,128)(2,1)}, bf16[6,2,8]{2,1,0:T(2,128)(2,1)}) custom-call(f32[12,1,128]{2,1,0:T(1,128)} %get-tuple-element.15.refs_0_, f32[12,1,128]{2,1,0:T(1,128)} %get-tuple-element.16.refs_1_, ...), custom_call_target="tpu_custom_call" | custom-call | tf_op jit(solution)/shard_map/place_results/pallas_call | solution.py:258

commit v2 on v1

--- a/solution.py
+++ b/solution.py
@@ -49,11 +49,16 @@
     return lax.fori_loop(1, count, body, carry)
 
 
+def arrived(slots, count, sem):
+    others = slots.at[pl.ds(1, count - 1)]
+    pltpu.make_async_copy(others, others, sem).wait()
+
+
 def kernel(
     n_inner, n_outer, rows, padded,
     grad_first, grad_second, master, first_moment, second_moment,
     new_master, new_first, new_second, weight_codes, weight_scales,
-    stage, terms, partial, sums, packed, state,
+    stage, terms, spread, partial, sums, packed, lined, state,
     load_sem, send_one, recv_one, send_two, recv_two, send_three, recv_three,
 ):
     inner = lax.axis_index("inner")
@@ -67,18 +72,6 @@
     def outer_peer(step):
         return lax.rem(outer + step, n_outer)
 
-    barrier = pltpu.get_barrier_semaphore()
-
-    def greet_inner(step, carry):
-        pl.semaphore_signal(barrier, inc=1, device_id={"inner": inner_peer(step)}, device_id_type=MESH)
-        return carry
-
-    def greet_outer(step, carry):
-        pl.semaphore_signal(barrier, inc=1, device_id={"outer": outer_peer(step)}, device_id_type=MESH)
-        return carry
-
-    loop(n_inner, greet_inner, 0)
-    loop(n_outer, greet_outer, 0)
     grads = [
         pltpu.make_async_copy(ref, stage.at[:, bucket], load_sem.at[bucket])
         for bucket, ref in enumerate((grad_first, grad_second))
@@ -87,114 +80,103 @@
         pltpu.make_async_copy(ref, state.at[place], load_sem.at[2 + place])
         for place, ref in enumerate((master, first_moment, second_moment))
     ]
-    for copy in grads + states:
+    for copy in grads:
+        copy.start()
+
+    barrier = pltpu.get_barrier_semaphore()
+
+    def greet_inner(step, carry):
+        pl.semaphore_signal(barrier, inc=1, device_id={"inner": inner_peer(step)}, device_id_type=MESH)
+        return carry
+
+    def greet_outer(step, carry):
+        pl.semaphore_signal(barrier, inc=1, device_id={"outer": outer_peer(step)}, device_id_type=MESH)
+        return carry
+
+    loop(n_inner, greet_inner, 0)
+    loop(n_outer, greet_outer, 0)
+    for copy in states:
         copy.start()
     for copy in grads:
         copy.wait()
     pl.semaphore_wait(barrier, n_inner - 1 + n_outer - 1)
 
-    def term_copy(step):
-        return pltpu.make_async_remote_copy(
+    def send_term(step, carry):
+        pltpu.make_async_remote_copy(
             src_ref=stage.at[inner_peer(step)],
             dst_ref=terms.at[step],
-            send_sem=send_one.at[step],
-            recv_sem=recv_one.at[step],
+            send_sem=send_one,
+            recv_sem=recv_one,
             device_id={"inner": inner_peer(step)},
             device_id_type=MESH,
-        )
-
-    def send_term(step, carry):
-        term_copy(step).start()
+        ).start()
         return carry
 
     loop(n_inner, send_term, 0)
     total = requantized(stage[inner].astype(jnp.float32))
-
-    def add_term(step, total):
-        term_copy(step).wait_recv()
-        return total + requantized(terms[step].astype(jnp.float32))
-
-    total = loop(n_inner, add_term, total).reshape(both, n_outer, width)
+    arrived(terms, n_inner, recv_one)
+    if n_inner <= 8:
+        total = total + jnp.sum(requantized(terms[1:].astype(jnp.float32)), axis=0)
+    else:
+        total = lax.fori_loop(
+            1, n_inner, lambda step, total: total + requantized(terms[step].astype(jnp.float32)), total
+        )
+    spread[...] = total.reshape(both * n_outer, width)
     for group in range(n_outer):
-        partial[group] = total[:, group]
-
-    def sum_copy(step):
-        return pltpu.make_async_remote_copy(
+        partial[group] = spread[pl.ds(group, both, stride=n_outer), :]
+
+    def send_sum(step, carry):
+        pltpu.make_async_remote_copy(
             src_ref=partial.at[outer_peer(step)],
             dst_ref=sums.at[step],
-            send_sem=send_two.at[step],
-            recv_sem=recv_two.at[step],
+            send_sem=send_two,
+            recv_sem=recv_two,
             device_id={"outer": outer_peer(step)},
             device_id_type=MESH,
-        )
-
-    def send_sum(step, carry):
-        sum_copy(step).start()
+        ).start()
         return carry
 
     loop(n_outer, send_sum, 0)
-    reduced = requantized(partial[outer])
+    own = requantized(partial[outer])
     for copy in states:
         copy.wait()
     params, first, second = (state[place, :, 0] for place in range(3))
-
-    def add_sum(step, reduced):
-        sum_copy(step).wait_recv()
-        return reduced + requantized(sums[step])
-
-    reduced = loop(n_outer, add_sum, reduced)
+    arrived(sums, n_outer, recv_two)
+    reduced = own + jnp.sum(requantized(sums[1:]), axis=0)
 
     params_next, first_next, second_next = adamw(reduced, params, first, second)
     codes, scale = quantize(params_next)
     lane = lax.broadcasted_iota(jnp.int32, (both, width), 1)
-    row = lax.broadcasted_iota(jnp.int32, (both, width), 0)
-    across = [
-        jnp.sum(jnp.where(lane + bucket * rows == row, jnp.where(lane < rows, scale, 0.0), 0.0), axis=0, keepdims=True)
-        for bucket in range(2)
-    ]
-    fill = jnp.zeros((padded - both - 2, width), jnp.float32)
-    packed[inner] = jnp.concatenate([codes] + across + [fill], axis=0).astype(jnp.bfloat16)
-
-    def weight_copy(step):
-        return pltpu.make_async_remote_copy(
+    across = jnp.where(lane == inner, scale, 0.0)
+    fill = jnp.zeros((padded - 2 * both, width), jnp.float32)
+    packed[inner] = jnp.concatenate([codes, across, fill], axis=0).astype(jnp.bfloat16)
+
+    def send_weight(step, carry):
+        pltpu.make_async_remote_copy(
             src_ref=packed.at[inner],
             dst_ref=packed.at[inner],
-            send_sem=send_three.at[step],
-            recv_sem=recv_three.at[step],
+            send_sem=send_three,
+            recv_sem=recv_three,
             device_id={"inner": inner_peer(step)},
             device_id_type=MESH,
-        )
-
-    def send_weight(step, carry):
-        weight_copy(step).start()
+        ).start()
         return carry
 
     loop(n_inner, send_weight, 0)
     new_master[:, 0] = params_next
     new_first[:, 0] = first_next
     new_second[:, 0] = second_next
-
-    def finish_terms(step, carry):
-        term_copy(step).wait_send()
-        return carry
-
-    def finish_sums(step, carry):
-        sum_copy(step).wait_send()
-        return carry
-
-    def finish_weights(step, carry):
-        weight_copy(step).wait()
-        return carry
-
-    loop(n_inner, finish_terms, 0)
-    loop(n_outer, finish_sums, 0)
-    loop(n_inner, finish_weights, 0)
+    arrived(terms, n_inner, send_one)
+    arrived(sums, n_outer, send_two)
+    arrived(packed, n_inner, send_three)
+    arrived(packed, n_inner, recv_three)
     gathered = packed[...].astype(jnp.float32)
+    lined[...] = gathered.reshape(n_inner * padded, width)
     for place in range(both):
-        weight_codes[place] = gathered[:, place].astype(jnp.bfloat16)
+        weight_codes[place] = lined[pl.ds(place, n_inner, stride=padded), :].astype(jnp.bfloat16)
+    scales = jnp.sum(gathered[:, both : 2 * both], axis=0)
     for bucket in range(2):
-        turned = jnp.transpose(gathered[:, both + bucket])
-        weight_scales[:, bucket] = turned[:rows].astype(jnp.bfloat16)
+        weight_scales[:, bucket] = scales[bucket * rows : (bucket + 1) * rows, :n_inner].astype(jnp.bfloat16)
 
 
 def place_kernel(*refs):
@@ -212,7 +194,7 @@
 def local(n_inner, n_outer, grad_first, grad_second, master, first_moment, second_moment):
     rows, width = grad_first.shape[-2:]
     both = 2 * rows
-    padded = 16 * ((both + 2 + 15) // 16)
+    padded = 16 * ((2 * both + 15) // 16)
     owned = jax.ShapeDtypeStruct((both, 1, width), jnp.float32)
     shapes = (
         owned,
@@ -230,27 +212,24 @@
         in_specs=[pl.BlockSpec(memory_space=pltpu.HBM)] * 5,
         out_specs=(vmem,) * 5,
         scratch_shapes=[
-            pltpu.VMEM((n_inner, 2, rows, n_outer, width), jnp.bfloat16),
-            pltpu.VMEM((n_inner, 2, rows, n_outer, width), jnp.bfloat16),
+            pltpu.VMEM((n_inner, 2, rows * n_outer, width), jnp.bfloat16),
+            pltpu.VMEM((n_inner, 2, rows * n_outer, width), jnp.bfloat16),
+            pltpu.VMEM((both * n_outer, width), jnp.float32),
             pltpu.VMEM((n_outer, both, width), jnp.float32),
             pltpu.VMEM((n_outer, both, width), jnp.float32),
             pltpu.VMEM((n_inner, padded, width), jnp.bfloat16),
+            pltpu.VMEM((n_inner * padded, width), jnp.float32),
             pltpu.VMEM((3, both, 1, width), jnp.float32),
             dma((5,)),
-            dma((n_inner,)),
-            dma((n_inner,)),
-            dma((n_outer,)),
-            dma((n_outer,)),
-            dma((n_inner,)),
-            dma((n_inner,)),
+            dma, dma, dma, dma, dma, dma,
         ],
         compiler_params=pltpu.CompilerParams(
             collective_id=0, has_side_effects=True
         ),
         name="reduce_update_gather",
     )(
-        jnp.swapaxes(grad_first[0, 0], 1, 2),
-        jnp.swapaxes(grad_second[0, 0], 1, 2),
+        jnp.swapaxes(grad_first[0, 0], 1, 2).reshape(n_inner, rows * n_outer, width),
+        jnp.swapaxes(grad_second[0, 0], 1, 2).reshape(n_inner, rows * n_outer, width),
         master.reshape(both, 1, width),
         first_moment.reshape(both, 1, width),
         second_moment.reshape(both, 1, width),

time: 19.6 us -> 19 us (0.969)
  Pallas kernels: 18.7 us -> 18.2 us
    pallas_call x1, Pallas kernels: 17.3 us -> 16.7 us  [local(): pl.pallas_call(functools.partial(kernel, n_inner, n_outer, rows, padded),...]
where the time goes in v2:
time: 19 us; the launch traced here: 18.8 us
  Pallas kernels  18.2 us (96%)
  between operations  0.64 us (3%)
    pallas_call x1, Pallas kernels, local(): pl.pallas_call(functools.partial(kernel, n_inner, n_outer, rows, padded),...  16.7 us
    pallas_call x1, Pallas kernels, local(): pl.pallas_call(place_kernel, out_shape=shapes, in_specs=[vmem] * 5, out_s...  1.42 us

profile of v2, /device:TPU:0, one launch (start us, length us, event | category | flops | bytes accessed | tf_op | source)
XLA Modules:
  0.0 18.8 jit_solution(3999169275749142672)
XLA Ops:
  0.6 16.7 %reduce_update_gather.1 = (f32[12,1,128]{2,1,0:T(1,128)}, f32[12,1,128]{2,1,0:T(1,128)}, f32[12,1,128]{2,1,0:T(1,128)}, bf16[12,8,128]{2,1,0:T(8,128)(2,1)}, bf16[6,2,8]{2,1,0:T(2,128)(2,1)}) custom-call(bf16[8,24,128]{2,1,0:T(8,128)(2,1)} %bitcast.30, bf16[8,24,128]{2,1,0:T(8,128)(2,1)} %bitcast.31, f32[12,1,128]{2,1,0:T(1,128)} %bitcast.32, ...), custom_call_target="tpu_custom_call" | custom-call | tf_op jit(solution)/shard_map/reduce_update_gather/pallas_call | solution.py:209
  17.4 1.4 %place_results.1 = (f32[12,1,128]{2,1,0:T(1,128)}, f32[12,1,128]{2,1,0:T(1,128)}, f32[12,1,128]{2,1,0:T(1,128)}, bf16[12,8,128]{2,1,0:T(8,128)(2,1)}, bf16[6,2,8]{2,1,0:T(2,128)(2,1)}) custom-call(f32[12,1,128]{2,1,0:T(1,128)} %get-tuple-element.15.refs_0_, f32[12,1,128]{2,1,0:T(1,128)} %get-tuple-element.16.refs_1_, ...), custom_call_target="tpu_custom_call" | custom-call | tf_op jit(solution)/shard_map/place_results/pallas_call | solution.py:237

commit v3 on v2

--- a/solution.py
+++ b/solution.py
@@ -49,6 +49,19 @@
     return lax.fori_loop(1, count, body, carry)
 
 
+def everyone(n_inner, n_outer, body):
+    if n_inner * n_outer <= 32:
+        for place in range(n_inner * n_outer - 1, 0, -1):
+            body(place // n_inner, place % n_inner)
+    else:
+
+        def step(place, carry):
+            body(place // n_inner, place % n_inner)
+            return carry
+
+        lax.fori_loop(1, n_inner * n_outer, step, 0)
+
+
 def arrived(slots, count, sem):
     others = slots.at[pl.ds(1, count - 1)]
     pltpu.make_async_copy(others, others, sem).wait()
@@ -58,8 +71,8 @@
     n_inner, n_outer, rows, padded,
     grad_first, grad_second, master, first_moment, second_moment,
     new_master, new_first, new_second, weight_codes, weight_scales,
-    stage, terms, spread, partial, sums, packed, lined, state,
-    load_sem, send_one, recv_one, send_two, recv_two, send_three, recv_three,
+    stage, spread, blocks, terms, packed, lined, state,
+    load_sem, send_one, recv_one, send_two, recv_two,
 ):
     inner = lax.axis_index("inner")
     outer = lax.axis_index("outer")
@@ -85,64 +98,54 @@
 
     barrier = pltpu.get_barrier_semaphore()
 
-    def greet_inner(step, carry):
-        pl.semaphore_signal(barrier, inc=1, device_id={"inner": inner_peer(step)}, device_id_type=MESH)
-        return carry
-
-    def greet_outer(step, carry):
-        pl.semaphore_signal(barrier, inc=1, device_id={"outer": outer_peer(step)}, device_id_type=MESH)
-        return carry
-
-    loop(n_inner, greet_inner, 0)
-    loop(n_outer, greet_outer, 0)
+    def greet(outer_step, inner_step):
+        peer = {"inner": inner_peer(inner_step), "outer": outer_peer(outer_step)}
+        pl.semaphore_signal(barrier, inc=1, device_id=peer, device_id_type=MESH)
+
+    everyone(n_inner, n_outer, greet)
     for copy in states:
         copy.start()
     for copy in grads:
         copy.wait()
-    pl.semaphore_wait(barrier, n_inner - 1 + n_outer - 1)
-
-    def send_term(step, carry):
+
+    spread[...] = stage[...].astype(jnp.float32).reshape(n_inner, both * n_outer, width)
+
+    def gather_rows(place, carry):
+        for group in range(n_outer):
+            blocks[place, group] = spread[place, pl.ds(group, both, stride=n_outer), :].astype(jnp.bfloat16)
+        return carry
+
+    gather_rows(0, 0)
+    loop(n_inner, gather_rows, 0)
+    pl.semaphore_wait(barrier, n_inner * n_outer - 1)
+
+    def send_term(outer_step, inner_step):
+        peer = {"inner": inner_peer(inner_step), "outer": outer_peer(outer_step)}
         pltpu.make_async_remote_copy(
-            src_ref=stage.at[inner_peer(step)],
-            dst_ref=terms.at[step],
+            src_ref=blocks.at[inner_peer(inner_step), outer_peer(outer_step)],
+            dst_ref=terms.at[outer_step * n_inner + inner_step],
             send_sem=send_one,
             recv_sem=recv_one,
-            device_id={"inner": inner_peer(step)},
+            device_id=peer,
             device_id_type=MESH,
         ).start()
-        return carry
-
-    loop(n_inner, send_term, 0)
-    total = requantized(stage[inner].astype(jnp.float32))
-    arrived(terms, n_inner, recv_one)
-    if n_inner <= 8:
-        total = total + jnp.sum(requantized(terms[1:].astype(jnp.float32)), axis=0)
-    else:
-        total = lax.fori_loop(
-            1, n_inner, lambda step, total: total + requantized(terms[step].astype(jnp.float32)), total
-        )
-    spread[...] = total.reshape(both * n_outer, width)
-    for group in range(n_outer):
-        partial[group] = spread[pl.ds(group, both, stride=n_outer), :]
-
-    def send_sum(step, carry):
-        pltpu.make_async_remote_copy(
-            src_ref=partial.at[outer_peer(step)],
-            dst_ref=sums.at[step],
-            send_sem=send_two,
-            recv_sem=recv_two,
-            device_id={"outer": outer_peer(step)},
-            device_id_type=MESH,
-        ).start()
-        return carry
-
-    loop(n_outer, send_sum, 0)
-    own = requantized(partial[outer])
+
+    everyone(n_inner, n_outer, send_term)
+    terms[0] = blocks[inner, outer]
     for copy in states:
         copy.wait()
     params, first, second = (state[place, :, 0] for place in range(3))
-    arrived(sums, n_outer, recv_two)
-    reduced = own + jnp.sum(requantized(sums[1:]), axis=0)
+    arrived(terms, n_inner * n_outer, recv_one)
+    if n_inner * n_outer <= 32:
+        arrivals = terms[...].astype(jnp.float32).reshape(n_outer, n_inner, both, width)
+        reduced = jnp.sum(requantized(jnp.sum(requantized(arrivals), axis=1)), axis=0)
+    else:
+
+        def add_group(group, reduced):
+            arrivals = terms[pl.ds(group * n_inner, n_inner)].astype(jnp.float32)
+            return reduced + requantized(jnp.sum(requantized(arrivals), axis=0))
+
+        reduced = lax.fori_loop(0, n_outer, add_group, jnp.zeros((both, width), jnp.float32))
 
     params_next, first_next, second_next = adamw(reduced, params, first, second)
     codes, scale = quantize(params_next)
@@ -155,8 +158,8 @@
         pltpu.make_async_remote_copy(
             src_ref=packed.at[inner],
             dst_ref=packed.at[inner],
-            send_sem=send_three,
-            recv_sem=recv_three,
+            send_sem=send_two,
+            recv_sem=recv_two,
             device_id={"inner": inner_peer(step)},
             device_id_type=MESH,
         ).start()
@@ -166,10 +169,9 @@
     new_master[:, 0] = params_next
     new_first[:, 0] = first_next
     new_second[:, 0] = second_next
-    arrived(terms, n_inner, send_one)
-    arrived(sums, n_outer, send_two)
-    arrived(packed, n_inner, send_three)
-    arrived(packed, n_inner, recv_three)
+    arrived(terms, n_inner * n_outer, send_one)
+    arrived(packed, n_inner, send_two)
+    arrived(packed, n_inner, recv_two)
     gathered = packed[...].astype(jnp.float32)
     lined[...] = gathered.reshape(n_inner * padded, width)
     for place in range(both):
@@ -213,15 +215,14 @@
         out_specs=(vmem,) * 5,
         scratch_shapes=[
             pltpu.VMEM((n_inner, 2, rows * n_outer, width), jnp.bfloat16),
-            pltpu.VMEM((n_inner, 2, rows * n_outer, width), jnp.bfloat16),
-            pltpu.VMEM((both * n_outer, width), jnp.float32),
-            pltpu.VMEM((n_outer, both, width), jnp.float32),
-            pltpu.VMEM((n_outer, both, width), jnp.float32),
+            pltpu.VMEM((n_inner, both * n_outer, width), jnp.float32),
+            pltpu.VMEM((n_inner, n_outer, both, width), jnp.bfloat16),
+            pltpu.VMEM((n_inner * n_outer, both, width), jnp.bfloat16),
             pltpu.VMEM((n_inner, padded, width), jnp.bfloat16),
             pltpu.VMEM((n_inner * padded, width), jnp.float32),
             pltpu.VMEM((3, both, 1, width), jnp.float32),
             dma((5,)),
-            dma, dma, dma, dma, dma, dma,
+            dma, dma, dma, dma,
         ],
         compiler_params=pltpu.CompilerParams(
             collective_id=0, has_side_effects=True

time: 19 us -> 18.5 us (0.974)
  Pallas kernels: 18.2 us -> 17.6 us
    pallas_call x1, Pallas kernels: 16.7 us -> 16.2 us  [local(): pl.pallas_call(functools.partial(kernel, n_inner, n_outer, rows, padded),...]
where the time goes in v3:
time: 18.5 us; the launch traced here: 18.2 us
  Pallas kernels  17.6 us (95%)
  between operations  0.64 us (3%)
    pallas_call x1, Pallas kernels, local(): pl.pallas_call(functools.partial(kernel, n_inner, n_outer, rows, padded),...  16.2 us
    pallas_call x1, Pallas kernels, local(): pl.pallas_call(place_kernel, out_shape=shapes, in_specs=[vmem] * 5, out_s...  1.42 us

profile of v3, /device:TPU:0, one launch (start us, length us, event | category | flops | bytes accessed | tf_op | source)
XLA Modules:
  0.0 18.2 jit_solution(5619980928147981146)
XLA Ops:
  0.6 16.2 %reduce_update_gather.1 = (f32[12,1,128]{2,1,0:T(1,128)}, f32[12,1,128]{2,1,0:T(1,128)}, f32[12,1,128]{2,1,0:T(1,128)}, bf16[12,8,128]{2,1,0:T(8,128)(2,1)}, bf16[6,2,8]{2,1,0:T(2,128)(2,1)}) custom-call(bf16[8,24,128]{2,1,0:T(8,128)(2,1)} %bitcast.30, bf16[8,24,128]{2,1,0:T(8,128)(2,1)} %bitcast.31, f32[12,1,128]{2,1,0:T(1,128)} %bitcast.32, ...), custom_call_target="tpu_custom_call" | custom-call | tf_op jit(solution)/shard_map/reduce_update_gather/pallas_call | solution.py:211
  16.8 1.4 %place_results.1 = (f32[12,1,128]{2,1,0:T(1,128)}, f32[12,1,128]{2,1,0:T(1,128)}, f32[12,1,128]{2,1,0:T(1,128)}, bf16[12,8,128]{2,1,0:T(8,128)(2,1)}, bf16[6,2,8]{2,1,0:T(2,128)(2,1)}) custom-call(f32[12,1,128]{2,1,0:T(1,128)} %get-tuple-element.15.refs_0_, f32[12,1,128]{2,1,0:T(1,128)} %get-tuple-element.16.refs_1_, ...), custom_call_target="tpu_custom_call" | custom-call | tf_op jit(solution)/shard_map/place_results/pallas_call | solution.py:238

commit v4 on v3

--- a/solution.py
+++ b/solution.py
@@ -79,11 +79,15 @@
     both = 2 * rows
     width = stage.shape[-1]
 
+    few = n_inner * n_outer <= 32
+    inner_peers = [lax.rem(inner + step, n_inner) for step in range(n_inner if few else 0)]
+    outer_peers = [lax.rem(outer + step, n_outer) for step in range(n_outer if few else 0)]
+
     def inner_peer(step):
-        return lax.rem(inner + step, n_inner)
+        return inner_peers[step] if few else lax.rem(inner + step, n_inner)
 
     def outer_peer(step):
-        return lax.rem(outer + step, n_outer)
+        return outer_peers[step] if few else lax.rem(outer + step, n_outer)
 
     grads = [
         pltpu.make_async_copy(ref, stage.at[:, bucket], load_sem.at[bucket])

time: 18.5 us -> 18.5 us (level)
  no operation moved by 1% of the time
where the time goes in v4:
time: 18.5 us; the launch traced here: 18.2 us
  Pallas kernels  17.6 us (95%)
  between operations  0.64 us (3%)
    pallas_call x1, Pallas kernels, local(): pl.pallas_call(functools.partial(kernel, n_inner, n_outer, rows, padded),...  16.2 us
    pallas_call x1, Pallas kernels, local(): pl.pallas_call(place_kernel, out_shape=shapes, in_specs=[vmem] * 5, out_s...  1.42 us

profile of v4, /device:TPU:0, one launch (start us, length us, event | category | flops | bytes accessed | tf_op | source)
XLA Modules:
  0.0 18.2 jit_solution(13260948253996913987)
XLA Ops:
  0.6 16.2 %reduce_update_gather.1 = (f32[12,1,128]{2,1,0:T(1,128)}, f32[12,1,128]{2,1,0:T(1,128)}, f32[12,1,128]{2,1,0:T(1,128)}, bf16[12,8,128]{2,1,0:T(8,128)(2,1)}, bf16[6,2,8]{2,1,0:T(2,128)(2,1)}) custom-call(bf16[8,24,128]{2,1,0:T(8,128)(2,1)} %bitcast.30, bf16[8,24,128]{2,1,0:T(8,128)(2,1)} %bitcast.31, f32[12,1,128]{2,1,0:T(1,128)} %bitcast.32, ...), custom_call_target="tpu_custom_call" | custom-call | tf_op jit(solution)/shard_map/reduce_update_gather/pallas_call | solution.py:215
  16.8 1.4 %place_results.1 = (f32[12,1,128]{2,1,0:T(1,128)}, f32[12,1,128]{2,1,0:T(1,128)}, f32[12,1,128]{2,1,0:T(1,128)}, bf16[12,8,128]{2,1,0:T(8,128)(2,1)}, bf16[6,2,8]{2,1,0:T(2,128)(2,1)}) custom-call(f32[12,1,128]{2,1,0:T(1,128)} %get-tuple-element.15.refs_0_, f32[12,1,128]{2,1,0:T(1,128)} %get-tuple-element.16.refs_1_, ...), custom_call_target="tpu_custom_call" | custom-call | tf_op jit(solution)/shard_map/place_results/pallas_call | solution.py:242
